TPU v7x, 32 devices: a whole 2x2x4 slice. The times are simulated.
32 devices in a mesh: groups: 2 (over y), leaf: 4 (over z), level: 2 (over x), sub: 2 (over core).
Axes of the slice: x: 2, y: 2, z: 4, core: 2. Of those that a mesh axis runs over, the one named last changes fastest.
Arguments:
- rhs: float32 [64, 262144], P(('level', 'sub'), ('groups', 'leaf')), parts along dimension 1, may hold values from -6 to 6
- points: float32 [3, 262144], P(None, ('groups', 'leaf')), parts along dimension 1, may hold values from 0 to 2
- basis: float32 [32, 262144], P(None, ('groups', 'leaf')), parts along dimension 1, may hold values from -0.75 to 0.75
- transfer: float32 [32, 261632], P(None, ('groups', 'leaf')), parts along dimension 1, may hold values from -0.875 to 0.875
- leaf_proxies: float32 [3, 131072], P(None, ('groups', 'leaf')), parts along dimension 1, may hold values from 0 to 2
- root_proxies: float32 [3, 256], P(None, 'groups'), parts along dimension 1, may hold values from 0 to 2
- near_src: int32 [4096, 8], P(('groups', 'leaf')), parts along dimension 0, may hold values from 0 to 2047, as said below
- near_count: int32 [4096], P(('groups', 'leaf')), parts along dimension 0, may hold values from 1 to 8, as said below
- far_src: int32 [4096, 16], P(('groups', 'leaf')), parts along dimension 0, may hold values from 0 to 2047, as said below
Outputs:
- product: float32 [64, 262144], P(('level', 'sub'), ('groups', 'leaf')), parts along dimension 1
There are 2 independent parts, one for each index of `groups`. A program takes and returns all parts, laid end to end along the dimension named above; each array names one. Nothing has to cross between parts.
Inputs may be any that keep to these rules, and one draw needn't show every extreme that they name: `near_src`: each entry of row t lies within 512 of t; in every draw some row names t + 512 and some row t - 512; entries may repeat. Entries 0 to near_count[t] - 1 of row t of near_src are live, the rest are ignored; some leaf has 8. `far_src`: each entry of row t lies within 512 of t; in every draw some row names t + 512 and some row t - 512; entries may repeat.
All inputs are finite; a program needn't handle non-finite values.
Results may differ from a plain program's by a relative error of at most 0.00017.
Values sent between devices are 32-bit elements; how exact they have to be, the bound alone decides.
No kernel may reach another device: no remote copies, remote signals or barrier semaphores. Data moves between devices by JAX's collectives and lax.ppermute only.
A program may use at most 192 MiB of HBM per device.

v0:
```python
import jax
import jax.numpy as jnp
from jax import lax
from jax.sharding import PartitionSpec as P

spread_sq = 0.5


def with_halo(shard, sides, width):
    for axis, dim in sides:
        size, length = (lax.axis_size(axis), shard.shape[dim])
        up = [(i, (i + 1) % size) for i in range(size - 1)]
        down = [(j, i) for i, j in up]
        last = lax.slice_in_dim(shard, length - width, length, axis=dim)
        leading = lax.slice_in_dim(shard, 0, width, axis=dim)
        before = lax.ppermute(last, axis, up)
        after = lax.ppermute(leading, axis, down)
        shard = jnp.concatenate([before, shard, after], axis=dim)
    return shard


def pair_rows(src_x, src_c, tgt_c, src_idx, live):
    rows = src_x.shape[0]
    count = tgt_c.shape[1]
    width = tgt_c.shape[2]
    listed = src_idx.shape[1]
    step = min(16, count)
    blocks = count // step
    source_table = jnp.moveaxis(jnp.concatenate([src_c, src_x], axis=0), 1, 0)
    tgt_blocks = jnp.moveaxis(tgt_c.reshape(3, blocks, step, width), 1, 0)
    idx_blocks = src_idx.reshape(blocks, step, listed)
    live_blocks = live.reshape(blocks, step, listed)

    def one_block(packed):
        tgt_here, idx_here, live_here = packed
        picked = jnp.take(source_table, idx_here.reshape(step * listed), axis=0)
        picked = picked.reshape(step, listed, rows + 3, width)
        picked = jnp.moveaxis(picked, 2, 0).reshape(rows + 3, step, listed * width)
        src_here = picked[:3]
        values = picked[3:]
        dist = (tgt_here[0][:, :, None] - src_here[0][:, None, :]) ** 2
        dist = dist + (tgt_here[1][:, :, None] - src_here[1][:, None, :]) ** 2
        dist = dist + (tgt_here[2][:, :, None] - src_here[2][:, None, :]) ** 2
        weight = jnp.repeat(live_here, width, axis=1)[:, None, :]
        kernel = jnp.exp(-dist / spread_sq) * weight
        return jnp.einsum("bij,rbj->rbi", kernel, values, precision=lax.Precision.HIGHEST)

    result = lax.map(one_block, (tgt_blocks, idx_blocks, live_blocks))
    return jnp.moveaxis(result, 0, 1).reshape(rows, count * width)


def local(rhs, points, basis, transfer, leaf_proxies, root_proxies, near_src, near_count, far_src):
    highest = lax.Precision.HIGHEST
    rows, width = rhs.shape
    leaves = near_src.shape[0]
    leaf_pts = width // leaves
    rank = basis.shape[0]
    near_max = near_src.shape[1]
    far_max = far_src.shape[1]
    levels = leaves.bit_length() - 1
    owner = lax.axis_index("leaf")
    anchor = owner * leaves - leaves
    rhs3 = rhs.reshape(rows, leaves, leaf_pts)
    basis3 = basis.reshape(rank, leaves, leaf_pts)
    coef = jnp.einsum("rlp,alp->rla", rhs3, basis3, precision=highest)
    point_rows = jnp.concatenate([rhs, points], axis=0)
    coef_rows = jnp.concatenate([coef.reshape(rows, leaves * rank), leaf_proxies], axis=0)
    ext_points = with_halo(point_rows, (("leaf", 1),), leaves * leaf_pts)
    ext_points = ext_points.reshape(rows + 3, 3 * leaves, leaf_pts)
    ext_coef = with_halo(coef_rows, (("leaf", 1),), leaves * rank)
    ext_coef = ext_coef.reshape(rows + 3, 3 * leaves, rank)
    near_local = near_src - anchor
    far_local = far_src - anchor
    live = (jnp.arange(near_max, dtype=jnp.int32)[None, :] < near_count[:, None]).astype(
        jnp.float32
    )
    own_points = points.reshape(3, leaves, leaf_pts)
    near = pair_rows(ext_points[:rows], ext_points[rows:], own_points, near_local, live)
    all_live = jnp.ones((leaves, far_max), jnp.float32)
    couple = pair_rows(
        ext_coef[:rows], ext_coef[rows:], leaf_proxies.reshape(3, leaves, rank), far_local, all_live
    )
    couple = couple.reshape(rows, leaves, rank)
    blocks = transfer.reshape(rank, 2 * leaves - 2, rank)
    mats = []
    current = coef
    for level in range(levels):
        here = leaves >> level
        offset = 2 * leaves - 2 * here
        mat = blocks[:, offset : offset + here, :]
        mats.append(mat)
        lifted = jnp.einsum("rca,acb->rcb", current, mat, precision=highest)
        current = lifted.reshape(rows, here // 2, 2, rank).sum(axis=2)
    root = current.reshape(rows, rank)
    own_proxy = lax.dynamic_slice_in_dim(root_proxies, owner * rank, rank, 1)
    piece = lax.all_gather(root, "leaf", axis=1, tiled=True)
    span = piece.shape[1]
    dist = (own_proxy[0][:, None] - root_proxies[0][None, :]) ** 2
    dist = dist + (own_proxy[1][:, None] - root_proxies[1][None, :]) ** 2
    dist = dist + (own_proxy[2][:, None] - root_proxies[2][None, :]) ** 2
    source_owner = jnp.arange(span, dtype=jnp.int32) // rank
    far_mask = (jnp.abs(source_owner - owner) >= 2).astype(jnp.float32)
    kernel = jnp.exp(-dist / spread_sq) * far_mask[None, :]
    down = jnp.einsum("aj,rj->ra", kernel, piece, precision=highest).reshape(rows, 1, rank)
    for level in reversed(range(levels)):
        down = jnp.einsum(
            "rcb,acb->rca", jnp.repeat(down, 2, axis=1), mats[level], precision=highest
        )
    down = down + couple
    far = jnp.einsum("rla,alp->rlp", down, basis3, precision=highest).reshape(rows, width)
    return near + far


def solution(mesh):
    in_specs = (
        P(("level", "sub"), ("groups", "leaf")),
        P(None, ("groups", "leaf")),
        P(None, ("groups", "leaf")),
        P(None, ("groups", "leaf")),
        P(None, ("groups", "leaf")),
        P(None, "groups"),
        P(("groups", "leaf"), None),
        P(("groups", "leaf")),
        P(("groups", "leaf"), None),
    )
    out_specs = P(("level", "sub"), ("groups", "leaf"))
    return jax.shard_map(local, mesh=mesh, in_specs=in_specs, out_specs=out_specs, check_vma=False)
```

profile of v0, /device:TPU:0, one launch (start us, length us, event | category | flops | bytes accessed | tf_op | source)
XLA Modules:
  0.0 1261.0 jit_solution(199523239879534635)
XLA Ops:
  5.5 7.3 collective-permute-start
  15.8 7.3 reshape.252
  23.1 24.7 %fusion.64 = f32[16,512,32]{2,0,1:T(8,128)S(1)} fusion(f32[16,512,64]{2,1,0:T(8,128)} %reshape.253, f32[32,512,64]{2,1,0:T(8,128)} %reshape.252), kind=kOutput, calls=%fused_computation.92 | convolution fusion | flops 201326592 | bytes 7340032 | tf_op jit(solution)/shard_map/rlp,alp->rla/dot_general | solution.py:65
  67.8 9.9 reshape.254
  79.3 7.5 slice.180
  105.6 25.1 %bitcast_reduce_fusion = f32[16,256,32]{2,0,1:T(8,128)S(1)} fusion(f32[16,512,32]{2,0,1:T(8,128)} %copy-done.3, f32[32,512,32]{2,1,0:T(8,128)} %slice.180), kind=kOutput, calls=%fused_computation.83 | convolution fusion | flops 100794368 | bytes 3670016 | tf_op jit(solution)/shard_map/rca,acb->rcb/dot_general | solution.py:92
  143.9 13.8 %all-gather = f32[4,32,16]{1,2,0:T(8,128)S(1)} all-gather(f32[1,32,16]{1,2,0:T(8,128)S(1)} %convolution_bitcast_fusion.7), channel_id=1, replica_groups=mesh['groups'=2,'leaf'=4,'level'=2,'sub'=2] {'leaf'}, dimensions={0}, use_global_device_ids=true | all-gather | bytes 10240 | tf_op jit(solution)/shard_map/all_gather | solution.py:96
  175.1 10.2 fusion.78
  187.3 9.4 slice.161
  196.7 7.5 copy.73
  216.4 11.8 copy.74
  228.3 487.8 %while.21 = (s32[]{:T(128)}, f32[32,16,16,32]{3,1,2,0:T(8,128)}, s32[32,16,16]{2,1,0:T(8,128)}, f32[1536,19,32]{2,1,0:T(8,128)}, f32[32,3,16,32]{3,2,0,1:T(8,128)}, /*index=5*/s32[]{:T(128)}) while((s32[]{:T(128)}, f32[32,16,16,32]{3,1,2,0:T(8,128)}, s32[32,16,16]{2,1,0:T(8,128)}, f32[1536,19,32]{2,1,0:T(8,128)}, ...), condition=%wide.region_11.12_spmd, body=%wide.region_10.11_spmd.sunk | while | flops 53112064 | bytes 8268405 | solution.py:48
  229.1 7.1 gather_fusion.1
  244.3 7.1 gather_fusion.1
  259.5 7.1 gather_fusion.1
  274.8 7.1 gather_fusion.1
  290.0 7.1 gather_fusion.1
  305.3 7.1 gather_fusion.1
  320.5 7.1 gather_fusion.1
  335.7 7.1 gather_fusion.1
  351.0 7.1 gather_fusion.1
  366.2 7.1 gather_fusion.1
  381.5 7.1 gather_fusion.1
  396.7 7.1 gather_fusion.1
  412.0 7.1 gather_fusion.1
  427.2 7.1 gather_fusion.1
  442.4 7.1 gather_fusion.1
  457.7 7.1 gather_fusion.1
  473.0 7.1 gather_fusion.1
  488.2 7.1 gather_fusion.1
  503.4 7.1 gather_fusion.1
  518.7 7.1 gather_fusion.1
  533.9 7.1 gather_fusion.1
  549.2 7.1 gather_fusion.1
  564.4 7.1 gather_fusion.1
  579.7 7.1 gather_fusion.1
  594.9 7.1 gather_fusion.1
  610.2 7.1 gather_fusion.1
  625.4 7.1 gather_fusion.1
  640.7 7.1 gather_fusion.1
  655.9 7.1 gather_fusion.1
  671.1 7.1 gather_fusion.1
  686.4 7.1 gather_fusion.1
  701.6 7.1 gather_fusion.1
  718.2 21.8 %bitcast_add_fusion = f32[16,512,32]{2,0,1:T(8,128)S(1)} fusion(f32[32,16,16,32]{3,1,2,0:T(8,128)} %get-tuple-element.65, f32[16,512,32]{2,0,1:T(8,128)S(1)} %bitcast.237, f32[32,512,32]{2,1,0:T(8,128)} %slice.180), kind=kOutput, calls=%fused_computation.82 | convolution fusion | flops 100925440 | bytes 5242880 | tf_op jit(solution)/shard_map/rcb,acb->rca/dot_general | solution.py:106
  740.0 12.7 %fusion.69 = f32[16,512,64]{2,0,1:T(8,128)S(1)} fusion(f32[16,512,32]{2,0,1:T(8,128)S(1)} %bitcast_add_fusion, f32[32,512,64]{2,1,0:T(8,128)S(1)} %bitcast.236), kind=kOutput, calls=%fused_computation.93 | convolution fusion | flops 201326592 | bytes 7340032 | tf_op jit(solution)/shard_map/rla,alp->rlp/dot_general | solution.py:110
  765.8 14.0 %slice.142 = f32[16,1536,64]{2,1,0:T(8,128)} reshape(f32[16,98304]{1,0:T(8,128)} %pad_maximum_fusion) | data formatting | bytes 12582912 | tf_op jit(solution)/shard_map/slice | solution.py:78
  791.2 24.6 %copy.55 = f32[1536,19,64]{2,1,0:T(8,128)} copy(f32[1536,19,64]{2,0,1:T(8,128)S(1)} %maximum_bitcast_fusion) | data formatting | bytes 14942208 | tf_op jit(solution)/shard_map/while | solution.py:48
  815.8 432.4 %while.20 = (s32[]{:T(128)}, f32[32,16,16,64]{3,1,2,0:T(8,128)}, s32[32,16,8]{1,0,2:T(8,128)}, f32[1536,19,64]{2,1,0:T(8,128)}, f32[32,3,16,64]{3,2,0,1:T(8,128)}, /*index=5*/f32[32,16,8]{1,2,0:T(8,128)S(1)}, s32[]{:T(128)}) while((s32[]{:T(128)}, f32[32,16,16,64]{3,1,2,0:T(8,128)}, s32[32,16,8]{1,0,2:T(8,128)}, f32[1536,19,64]{2,1,0:T(8,128)}, ...), condition=%wide.region_1.2_spmd, body=%wide.region_0.1_spmd.sunk | while | flops 106588288 | bytes 5939813 | solution.py:48
  816.8 7.0 gather_fusion
  830.3 7.0 gather_fusion
  951.9 7.0 gather_fusion
  978.9 7.0 gather_fusion
  992.4 7.0 gather_fusion
  1005.9 7.0 gather_fusion
  1046.4 7.0 gather_fusion
  1087.0 7.0 gather_fusion
  1100.5 7.0 gather_fusion
  1114.0 7.0 gather_fusion
  1127.5 7.0 gather_fusion
  1154.5 7.0 gather_fusion
  1168.1 7.0 gather_fusion
  1208.6 7.0 gather_fusion
  1222.1 7.0 gather_fusion
  (1302 shorter events, 715.5 us)
Async XLA Ops:
  0.0 12.8 %copy-start.5 = (f32[16,32768]{1,0:T(8,128)S(1)}, f32[16,32768]{1,0:T(8,128)}, u32[]{:S(2)}) copy-start(f32[16,32768]{1,0:T(8,128)} %param.13) | copy-start | bytes 6291460
  0.0 3.2 copy-start.7
  4.2 755.7 %collective-permute-start.1 = (f32[19,32768]{1,0:T(8,128)}, f32[19,32768]{1,0:T(8,128)}, u32[]{:S(2)}, u32[]{:S(2)}) collective-permute-start(f32[19,32768]{1,0:T(8,128)} %constant_dynamic-update-slice_fusion), channel_id=1, source_target_pairs={{4,0},{8,4},{12,8},{5,1},{9,5},{13,9},{6,2},{10,6},{14,10},{7,3},{... | collective-permute-start | bytes 7471112 | tf_op jit(solution)/shard_map/ppermute | solution.py:17
  5.5 754.4 %collective-permute-start = (f32[19,32768]{1,0:T(8,128)}, f32[19,32768]{1,0:T(8,128)}, u32[]{:S(2)}, u32[]{:S(2)}) collective-permute-start(f32[19,32768]{1,0:T(8,128)} %constant_dynamic-update-slice_fusion), channel_id=1, source_target_pairs={{0,4},{4,8},{8,12},{1,5},{5,9},{9,13},{2,6},{6,10},{10,14},{3,7},{... | collective-permute-start | bytes 7471112 | tf_op jit(solution)/shard_map/ppermute | solution.py:16
  47.8 1.9 copy-start.3
  53.0 4.6 copy-start.8
  58.4 126.9 %collective-permute-start.3 = (f32[19,16384]{1,0:T(8,128)}, f32[19,16384]{1,0:T(8,128)}, u32[]{:S(2)}, u32[]{:S(2)}) collective-permute-start(f32[19,16384]{1,0:T(8,128)} %constant_dynamic-update-slice_fusion.2), channel_id=1, source_target_pairs={{4,0},{8,4},{12,8},{5,1},{9,5},{13,9},{6,2},{10,6},{14,10},{7,3},{... | collective-permute-start | bytes 3735560 | tf_op jit(solution)/shard_map/ppermute | solution.py:17
  59.7 125.6 %collective-permute-start.2 = (f32[19,16384]{1,0:T(8,128)}, f32[19,16384]{1,0:T(8,128)}, u32[]{:S(2)}, u32[]{:S(2)}) collective-permute-start(f32[19,16384]{1,0:T(8,128)} %constant_dynamic-update-slice_fusion.2), channel_id=1, source_target_pairs={{0,4},{4,8},{8,12},{1,5},{5,9},{9,13},{2,6},{6,10},{10,14},{3,7},{... | collective-permute-start | bytes 3735560 | tf_op jit(solution)/shard_map/ppermute | solution.py:16
  105.6 25.1 %copy-start.1 = (f32[32,256,32]{2,1,0:T(8,128)S(1)}, f32[32,256,32]{2,1,0:T(8,128)}, u32[]{:S(2)}) copy-start(f32[32,256,32]{2,1,0:T(8,128)} %slice.181) | copy-start | bytes 3145732
  136.8 4.8 copy-start.6
  136.8 6.7 copy-start.9
  136.8 6.9 copy-start.10
  170.5 4.6 copy-start.2
  236.8 1.4 copy-start
  252.1 1.4 copy-start
  267.3 1.4 copy-start
  282.5 1.4 copy-start
  297.8 1.4 copy-start
  313.0 1.4 copy-start
  328.3 1.4 copy-start
  343.5 1.4 copy-start
  358.7 1.4 copy-start
  374.0 1.4 copy-start
  389.2 1.4 copy-start
  404.5 1.4 copy-start
  419.7 1.4 copy-start
  434.9 1.4 copy-start
  450.2 1.4 copy-start
  465.5 1.4 copy-start
  480.7 1.4 copy-start
  496.0 1.4 copy-start
  511.2 1.4 copy-start
  526.4 1.4 copy-start
  541.7 1.4 copy-start
  556.9 1.4 copy-start
  572.2 1.4 copy-start
  587.4 1.4 copy-start
  602.7 1.4 copy-start
  617.9 1.4 copy-start
  633.2 1.4 copy-start
  648.4 1.4 copy-start
  663.7 1.4 copy-start
  678.9 1.4 copy-start
  694.1 1.4 copy-start
  709.4 1.4 copy-start
  716.1 23.9 %slice-start = ((s8[8388608]{0:T(1024)(128)(4,1)}), s8[4194304]{0:T(1024)(128)(4,1)S(1)}, s32[]{:S(2)}) async-start(s8[8388608]{0:T(1024)(128)(4,1)} %bitcast.235), calls=%async_computation | async-start | bytes 8388608
  718.2 21.9 %slice-start.1 = ((s8[8388608]{0:T(1024)(128)(4,1)}), s8[4194304]{0:T(1024)(128)(4,1)S(1)}, s32[]{:S(2)}) async-start(s8[8388608]{0:T(1024)(128)(4,1)} %bitcast.235), calls=%async_computation.1 | async-start | bytes 8388608
  1253.7 4.0 copy-start.4
where the time goes:
time: 1280 us; the launch traced here: 1260 us
  local copies, waits for them, and re-layouts  849 us (66%)
  matrix products  297 us (23%)
  other arithmetic  81.8 us (6%)
  starting transfers between devices  15.6 us (1%)
  blocking collectives  13.8 us (1%)
    gather x64, local copies, waits for them, and re-layouts, one_block(): picked = jnp.take(source_table, idx_here.reshape(step * listed), axis=0)  453 us
    dot_general x64, matrix products, one_block(): jnp.einsum('bij,rbj->rbi', kernel, values, precision=lax.Precision.HIGHEST)  177 us
    dynamic_slice x128, local copies, waits for them, and re-layouts, pair_rows(): result = lax.map(one_block, (tgt_blocks, idx_blocks, live_blocks))  74.4 us
    while x64, local copies, waits for them, and re-layouts  45.6 us
    slice x128, local copies, waits for them, and re-layouts, one_block(): values = picked[3:]  45.1 us
    dot_general x9, matrix products, local(): jnp.einsum('rcb,acb->rca', jnp.repeat(down, 2, axis=1), mats[level], prec...  43.8 us
    dot_general x9, matrix products, local(): lifted = jnp.einsum('rca,acb->rcb', current, mat, precision=highest)  38.1 us
    while x2, local copies, waits for them, and re-layouts, pair_rows(): result = lax.map(one_block, (tgt_blocks, idx_blocks, live_blocks))  36.4 us
  transfers between devices with their start and end apart: 4, of which 0 were waited for; matrix products, arithmetic and copies ran while one was open for 54% of the time, Pallas kernels for 0%

commit v1 on v0

v1 whole, which is shorter than its diff:
```python
import functools
import math

import jax
import jax.numpy as jnp
import numpy as np
from jax import lax
from jax.experimental import pallas as pl
from jax.experimental.pallas import tpu as pltpu
from jax.sharding import PartitionSpec as P

spread_sq = 0.5
LANES = 128
FEATS = 16
UNROLL = 32
WIDE = 2
VMEM_LIMIT = 58 * 1024 * 1024
f32, bf16, i32 = jnp.float32, jnp.bfloat16, jnp.int32

NN = (((1,), (0,)), ((), ()))
NT = (((1,), (1,)), ((), ()))


def dot(a, b, dims=NN):
    return lax.dot_general(a, b, dims, preferred_element_type=f32)


def halves(x):
    hi = x.astype(bf16).astype(f32)
    return hi, x - hi


def stacked(x):
    hi, lo = halves(x)
    return jnp.concatenate([hi, lo], axis=0).astype(bf16)


def two_term(x, terms, dims):
    rows = x.shape[0]
    xs = stacked(x)
    high = dot(xs, terms[0], dims)
    low = dot(xs, terms[1], dims)
    return (high[:rows] + high[rows:]) + (low[:rows] + low[rows:])


def in_chunks(count, most, run):
    size = min(count, most)
    if count == size:
        run(0, size)
    else:

        def step(i, carry):
            run(i * size, size)
            return carry

        lax.fori_loop(0, count // size, step, 0)


def at(i, size):
    first = i * size
    return pl.ds(first if isinstance(first, int) else pl.multiple_of(first, size), size)


def span_of(first, n):
    start = first * LANES
    return pl.ds(start if isinstance(start, int) else pl.multiple_of(start, LANES), n * LANES)


def group_mask(shape, row_width, col_width):
    row = lax.broadcasted_iota(i32, shape, 0) // row_width
    col = lax.broadcasted_iota(i32, shape, 1) // col_width
    return row == col


def spread_rows(mat, copies, mask):
    zero = jnp.zeros((), bf16)
    parts = [part.astype(bf16) for part in halves(mat)]
    return [jnp.where(mask, jnp.concatenate([part] * copies, axis=0), zero) for part in parts]


def whole(n):
    return [pl.BlockSpec(memory_space=pltpu.VMEM)] * n


def call(body, out_shape, n_in, scratch=(), flops=0, nbytes=0, prefetch=False):
    specs = ([pl.BlockSpec(memory_space=pltpu.SMEM)] if prefetch else []) + whole(n_in)
    return pl.pallas_call(
        body,
        out_shape=out_shape,
        in_specs=specs,
        out_specs=pl.BlockSpec(memory_space=pltpu.VMEM),
        scratch_shapes=list(scratch),
        compiler_params=pltpu.CompilerParams(vmem_limit_bytes=VMEM_LIMIT),
        cost_estimate=pl.CostEstimate(flops=flops, bytes_accessed=nbytes, transcendentals=0),
    )


def leaf_coefs(rhs, basis, leaf_pts):
    rows, width = rhs.shape
    rank = basis.shape[0]
    per = LANES // rank
    span = per * leaf_pts

    def body(x_ref, b_ref, o_ref):
        mask = group_mask((per * rank, span), rank, leaf_pts)

        def run(first, n):
            ids = [first + j for j in range(n)]
            ins = [(x_ref[:, at(i, span)], b_ref[:, at(i, span)]) for i in ids]
            outs = [two_term(x, spread_rows(m, per, mask), NT) for x, m in ins]
            for i, out in zip(ids, outs):
                o_ref[:, at(i, LANES)] = out

        in_chunks(width // span, 8, run)

    out = jax.ShapeDtypeStruct((rows, width // leaf_pts * rank), f32)
    return call(body, out, 2, flops=10**9, nbytes=4 * width * (rows + rank))(rhs, basis)


def leaf_product(down, couple, basis, near, leaf_pts):
    rows, width = near.shape
    rank = basis.shape[0]
    per = LANES // rank
    span = per * leaf_pts

    def body(d_ref, c_ref, b_ref, n_ref, o_ref):
        mask = group_mask((per * rank, span), rank, leaf_pts)

        def run(first, n):
            ids = [first + j for j in range(n)]
            ins = [
                (d_ref[:, at(i, LANES)] + c_ref[:, at(i, LANES)], b_ref[:, at(i, span)]) for i in ids
            ]
            outs = [two_term(x, spread_rows(m, per, mask), NN) for x, m in ins]
            for i, out in zip(ids, outs):
                o_ref[:, at(i, span)] = n_ref[:, at(i, span)] + out

        in_chunks(width // span, 8, run)

    out = jax.ShapeDtypeStruct((rows, width), f32)
    return call(body, out, 4, flops=10**9, nbytes=4 * width * (3 * rows + rank))(
        down, couple, basis, near
    )


def tree_up(coef, transfer, leaves):
    rows, width = coef.shape
    rank = transfer.shape[0]
    levels = leaves.bit_length() - 1

    def body(c_ref, e_ref, o_ref, buf):
        for level in range(levels):
            here = leaves >> level
            offset = (2 * leaves - 2 * here) * rank
            share = 1 if level == 0 else 2
            out_span = min(LANES, here * rank)
            groups = out_span // rank * share
            span = groups * rank
            mask = group_mask((span, out_span), share * rank, rank)
            src = c_ref if level == 0 else buf.at[(level - 1) % 2]
            dst = buf.at[level % 2]

            def run(first, n):
                ids = [first + j for j in range(n)]
                base = offset // out_span
                ins = [(src[:, at(i, span)], e_ref[:, at(base + i, out_span)]) for i in ids]
                outs = [two_term(x, spread_rows(m, groups, mask), NN) for x, m in ins]
                for i, out in zip(ids, outs):
                    dst[:, at(i, out_span)] = out

            in_chunks(here * rank // out_span, 8, run)
        last = buf[(levels - 1) % 2, :, : 2 * rank]
        o_ref[...] = last[:, :rank] + last[:, rank:]

    return call(
        body,
        jax.ShapeDtypeStruct((rows, rank), f32),
        2,
        [pltpu.VMEM((2, rows, width), f32)],
        flops=10**9,
        nbytes=4 * width * (rows + 2 * rank),
    )(coef, transfer)


def tree_down(root, transfer, leaves):
    rows = root.shape[0]
    rank = transfer.shape[0]
    levels = leaves.bit_length() - 1
    width = leaves * rank

    def body(r_ref, e_ref, o_ref, buf):
        top = r_ref[...]
        buf[levels % 2, :, : 2 * rank] = jnp.concatenate([top, top], axis=1)
        for level in reversed(range(levels)):
            here = leaves >> level
            offset = (2 * leaves - 2 * here) * rank
            share = 1 if level == 0 else 2
            in_span = min(LANES, here * rank)
            groups = in_span // rank * share
            span = groups * rank
            mask = group_mask((span, in_span), share * rank, rank)
            src = buf.at[(level + 1) % 2]
            dst = o_ref if level == 0 else buf.at[level % 2]

            def run(first, n):
                ids = [first + j for j in range(n)]
                base = offset // in_span
                ins = [(src[:, at(i, in_span)], e_ref[:, at(base + i, in_span)]) for i in ids]
                outs = [two_term(x, spread_rows(m, groups, mask), NT) for x, m in ins]
                for i, out in zip(ids, outs):
                    dst[:, at(i, span)] = out

            in_chunks(here * rank // in_span, 8, run)

    return call(
        body,
        jax.ShapeDtypeStruct((rows, width), f32),
        2,
        [pltpu.VMEM((2, rows, width), f32)],
        flops=10**9,
        nbytes=4 * width * (rows + 2 * rank),
    )(root, transfer)


LOG2E = math.log2(math.e)


def selections():
    source, target = np.zeros((FEATS, FEATS), np.float32), np.zeros((FEATS, FEATS), np.float32)
    for d in range(3):
        for row, (p, q) in enumerate(((0, 0), (0, 1), (1, 0), (1, 1))):
            target[3 * row + d, 8 * p + d] = 1.0
            source[3 * row + d, 8 * q + d] = 1.0
    for row, term in ((12, 3), (13, 11)):
        source[row, term] = 1.0
        target[row, 4] = 1.0
        target[row + 2, term] = 1.0
        source[row + 2, 4] = 1.0
    return source, target


def features(coords, selection, scale):
    c = coords - 1.0
    row = lax.broadcasted_iota(i32, c.shape, 0)
    square = (-LOG2E / spread_sq) * jnp.sum(c * c, axis=0, keepdims=True)
    terms = jnp.where(row == 3, square, jnp.where(row == 4, 1.0, c * scale))
    return dot(selection, stacked(terms))


def eight_rows(coords):
    return jnp.pad(coords, ((0, 5), (0, 0)), constant_values=1.0)


def work_list(idx, live, group, dummy):
    count, listed = idx.shape
    items = count * (listed // group)
    livei = live.astype(i32)
    rank = jnp.sum(
        livei[:, None, :] * (jnp.arange(listed)[None, None, :] < jnp.arange(listed)[None, :, None]),
        axis=2,
    )
    slot = jnp.arange(listed, dtype=i32)
    hit = live[:, :, None] & (rank[:, :, None] == slot[None, None, :])
    total = jnp.sum(livei, axis=1)
    packed = jnp.sum(jnp.where(hit, idx[:, :, None], 0), axis=1)
    packed = jnp.where(slot[None, :] < total[:, None], packed, dummy)
    need = (total + group - 1) // group
    upto = jnp.arange(count)
    start = jnp.sum(jnp.where(upto[None, :] < upto[:, None], need[None, :], 0), axis=1)
    end = start + need
    k = jnp.arange(items, dtype=i32)
    one_hot = (start[None, :] <= k[:, None]) & (k[:, None] < end[None, :])
    target = jnp.sum(jnp.where(one_hot, upto[None, :].astype(i32), 0), axis=1)
    within = jnp.sum(jnp.where(one_hot, k[:, None] - start[None, :], 0), axis=1)
    rows = jnp.einsum(
        "kt,tm->km", one_hot.astype(f32), packed.astype(f32), precision=lax.Precision.HIGHEST
    )
    rows = jnp.round(rows).astype(i32).reshape(items, listed // group, group)
    pick = within[:, None, None] == jnp.arange(listed // group)[None, :, None]
    sources = jnp.sum(jnp.where(pick, rows, 0), axis=1)
    used = jnp.sum(need)
    sources = jnp.where((k < used)[:, None], sources, dummy)
    steps = (used + UNROLL - 1) // UNROLL
    return jnp.concatenate([target, sources.T.reshape(-1), steps[None]]), items


def pair_sums(listing, items, place, coords, sources, before, leaves, pts):
    rows = sources[0].shape[0]
    width = leaves * pts
    per = LANES // pts
    pieces = len(sources)
    held = pieces * leaves
    group = WIDE * per
    narrow = per > 2
    pick_source, pick_target = selections()
    eye = np.eye(LANES, dtype=np.float32)
    consts = [jnp.asarray(m, bf16) for m in (pick_source, pick_target, eye)]

    def body(list_ref, pick_s_ref, pick_t_ref, eye_ref, place_ref, *refs):
        coord_refs = refs[:pieces]
        x_refs = refs[pieces : 2 * pieces]
        more = refs[2 * pieces :]
        base_ref = more[0] if before is not None else None
        o_ref, tab, targets_tab, acc = more[-4:]
        lane = lax.broadcasted_iota(i32, (1, LANES), 1) // pts

        def fill_targets(first, n):
            here = span_of(first, n)
            feats = features(place_ref[:, here], pick_t_ref[...], 2.0 * LOG2E / spread_sq).astype(bf16)
            outs = [
                dot(eye_ref[...], feats[:, j * LANES : (j + 1) * LANES], NT).astype(bf16)
                for j in range(n)
            ]
            for j, out in enumerate(outs):
                for g in range(per):
                    targets_tab[(first + j) * per + g] = out[g * pts : (g + 1) * pts]

        in_chunks(width // LANES, 32, fill_targets)

        for piece in range(pieces):

            def fill(first, n):
                here = span_of(first, n)
                feats = features(coord_refs[piece][:, here], pick_s_ref[...], 1.0)
                hi, lo = halves(x_refs[piece][:, here])
                whole_rec = jnp.concatenate([feats, hi, lo], axis=0)
                outs = []
                for c in range(n):
                    rec = whole_rec[:, c * LANES : (c + 1) * LANES]
                    turned = [rec] + [pltpu.roll(rec, pts * j, 1) for j in range(1, per)]
                    for j in range(per):
                        out = turned[(per - j) % per]
                        for g in range(1, per):
                            out = jnp.where(lane == g, turned[(g - j) % per], out)
                        outs.append(out.astype(bf16))
                for j, out in enumerate(outs):
                    tab[piece * leaves + first * per + j] = out

            in_chunks(width // LANES, 16, fill)
        tab[held] = jnp.zeros(tab.shape[1:], bf16)

        def clear(first, n):
            for j in range(n):
                acc[first + j] = jnp.zeros(acc.shape[1:], f32)

        in_chunks(leaves, 32, clear)

        masks = [
            lax.broadcasted_iota(i32, (FEATS + 2 * rows, LANES), 1) >= g * pts
            for g in range(1, per)
        ]

        def step(n, carry):
            ks = [n * UNROLL + u for u in range(UNROLL)]
            targets = [list_ref[k] for k in ks]
            recs = []
            for k in ks:
                blocks = []
                for w in range(WIDE):
                    rec = tab[list_ref[(w * per + 1) * items + k]]
                    for g in range(1, per):
                        other = tab[list_ref[(w * per + g + 1) * items + k]]
                        rec = jnp.where(masks[g - 1], other, rec)
                    blocks.append(rec)
                recs.append(jnp.concatenate(blocks, axis=1))
            logs = [dot(targets_tab[t], rec[:FEATS]) for t, rec in zip(targets, recs)]
            kernels = [jnp.exp2(e) for e in logs]
            his = [k.astype(bf16) for k in kernels]
            los = [(k - h.astype(f32)).astype(bf16) for k, h in zip(kernels, his)]
            outs = []
            for rec, hi, lo in zip(recs, his, los):
                both = jnp.concatenate([hi, lo], axis=0)
                if narrow:
                    out = dot(both, rec[FEATS:], NT)
                    outs.append(out[:pts] + out[pts:])
                else:
                    out = dot(rec[FEATS:], both, NT)
                    outs.append(out[:rows] + out[rows:])
            for t, out in zip(targets, outs):
                acc[t] += out
            return carry

        lax.fori_loop(0, list_ref[(group + 1) * items], step, 0)

        def lay(start, n):
            outs = []
            for c in range(n):
                first = (start + c) * per
                if narrow:
                    out = jnp.concatenate([acc[first + j] for j in range(per)], axis=0).T
                    outs.append(out[:rows] + out[rows:])
                else:
                    for j in range(per):
                        one = acc[first + j]
                        one = one + pltpu.roll(one, pts, 1)
                        out = one if j == 0 else jnp.where(lane == j, one, out)
                    outs.append(out)
            for c, out in enumerate(outs):
                here = at(start + c, LANES)
                o_ref[:, here] = out if base_ref is None else out + base_ref[:, here]

        in_chunks(width // LANES, 16, lay)

    scratch = [
        pltpu.VMEM((held + 1, FEATS + 2 * rows, LANES), bf16),
        pltpu.VMEM((leaves, pts, FEATS), bf16),
        pltpu.VMEM((leaves, pts, 2 * rows) if narrow else (leaves, rows, LANES), f32),
    ]
    args = [listing, *consts, place, *coords, *sources] + ([before] if before is not None else [])
    return call(
        body,
        jax.ShapeDtypeStruct((rows, width), f32),
        len(args) - 1,
        scratch,
        flops=4 * 10**9,
        nbytes=3 * 10**7,
        prefetch=True,
    )(*args)


def local(rhs, points, basis, transfer, leaf_proxies, root_proxies, near_src, near_count, far_src):
    highest = lax.Precision.HIGHEST
    rows, width = rhs.shape
    leaves = near_src.shape[0]
    leaf_pts = width // leaves
    rank = basis.shape[0]
    near_max = near_src.shape[1]
    owner = lax.axis_index("leaf")
    size = lax.axis_size("leaf")
    up = [(i, (i + 1) % size) for i in range(size - 1)]
    down_pairs = [(j, i) for i, j in up]
    both_ways = lambda x: (lax.ppermute(x, "leaf", up), lax.ppermute(x, "leaf", down_pairs))

    shares = lax.axis_size("level") * lax.axis_size("sub")
    mine = lax.axis_index("level") * lax.axis_size("sub") + lax.axis_index("sub")
    near_share, far_share = width // shares, leaves * rank // shares
    share = jnp.concatenate(
        [
            lax.dynamic_slice_in_dim(points, mine * near_share, near_share, 1),
            lax.dynamic_slice_in_dim(leaf_proxies, mine * far_share, far_share, 1),
        ],
        axis=1,
    )
    share = jnp.stack(both_ways(share))
    coords = lax.all_gather(share, ("level", "sub"), axis=0)
    coords = jnp.moveaxis(coords, 0, 2)
    halo_points = coords[..., :near_share].reshape(2, 3, width)
    halo_proxies = coords[..., near_share:].reshape(2, 3, leaves * rank)

    coef = leaf_coefs(rhs, basis, leaf_pts)
    halo_rhs = both_ways(rhs)
    halo_coef = both_ways(coef)

    anchor = owner * leaves

    def lists(src, live, group):
        place = src - anchor
        own = (place >= 0) & (place < leaves)
        inside = work_list(place, live & own, group, leaves)
        outside = jnp.where(place < 0, place + leaves, place)
        return inside, work_list(outside, live & ~own, group, 2 * leaves)

    live = jnp.arange(near_max, dtype=i32)[None, :] < near_count[:, None]
    near_in, near_out = lists(near_src, live, WIDE * LANES // leaf_pts)
    far_in, far_out = lists(far_src, jnp.ones(far_src.shape, bool), WIDE * LANES // rank)

    own_points, own_proxies = eight_rows(points), eight_rows(leaf_proxies)
    near = pair_sums(*near_in, own_points, [own_points], [rhs], None, leaves, leaf_pts)
    couple = pair_sums(*far_in, own_proxies, [own_proxies], [coef], None, leaves, rank)

    root = tree_up(coef, transfer, leaves)
    own_proxy = lax.dynamic_slice_in_dim(root_proxies, owner * rank, rank, 1)
    piece = lax.all_gather(root, "leaf", axis=1, tiled=True)
    dist = (own_proxy[0][:, None] - root_proxies[0][None, :]) ** 2
    dist = dist + (own_proxy[1][:, None] - root_proxies[1][None, :]) ** 2
    dist = dist + (own_proxy[2][:, None] - root_proxies[2][None, :]) ** 2
    source_owner = jnp.arange(piece.shape[1], dtype=i32) // rank
    far_mask = (jnp.abs(source_owner - owner) >= 2).astype(f32)
    kernel = jnp.exp(-dist / spread_sq) * far_mask[None, :]
    top = jnp.einsum("aj,rj->ra", kernel, piece, precision=highest)
    down = tree_down(top, transfer, leaves)

    halo_points = [eight_rows(halo_points[i]) for i in range(2)]
    halo_proxies = [eight_rows(halo_proxies[i]) for i in range(2)]
    near = pair_sums(*near_out, own_points, halo_points, list(halo_rhs), near, leaves, leaf_pts)
    couple = pair_sums(
        *far_out, own_proxies, halo_proxies, list(halo_coef), couple, leaves, rank
    )
    return leaf_product(down, couple, basis, near, leaf_pts)


def solution(mesh):
    in_specs = (
        P(("level", "sub"), ("groups", "leaf")),
        P(None, ("groups", "leaf")),
        P(None, ("groups", "leaf")),
        P(None, ("groups", "leaf")),
        P(None, ("groups", "leaf")),
        P(None, "groups"),
        P(("groups", "leaf"), None),
        P(("groups", "leaf")),
        P(("groups", "leaf"), None),
    )
    out_specs = P(("level", "sub"), ("groups", "leaf"))
    return jax.shard_map(local, mesh=mesh, in_specs=in_specs, out_specs=out_specs, check_vma=False)
```

time: 1280 us -> 277 us (0.22)
  the two profiles are of different devices: /device:TPU:0 before, /device:TPU:20 now
where the time goes in v1:
time: 277 us; the launch traced here: 274 us
  Pallas kernels  183 us (66%)
  blocking collectives  25.6 us (9%)
  starting transfers between devices  18.8 us (7%)
  between operations  16.4 us (6%)
  other arithmetic  13.1 us (5%)
  local copies, waits for them, and re-layouts  11.8 us (4%)
  matrix products  5.67 us (2%)
    pallas_call x4, Pallas kernels, pair_sums(): call(body, jax.ShapeDtypeStruct((rows, width), f32), len(args) - 1, scrat...  134 us
    all_gather x1, blocking collectives, local(): piece = lax.all_gather(root, 'leaf', axis=1, tiled=True)  25.6 us
    pallas_call x1, Pallas kernels, tree_down(): call(body, jax.ShapeDtypeStruct((rows, width), f32), 2, [pltpu.VMEM((2, r...  17 us
    pallas_call x1, Pallas kernels, tree_up(): call(body, jax.ShapeDtypeStruct((rows, rank), f32), 2, [pltpu.VMEM((2, ro...  12.1 us
    ppermute x3, starting transfers between devices, local(): lax.ppermute(x, 'leaf', up)  12 us
    pallas_call x1, Pallas kernels, leaf_coefs(): call(body, out, 2, flops=10 ** 9, nbytes=4 * width * (rows + rank))  10.9 us
    pallas_call x1, Pallas kernels, leaf_product(): call(body, out, 4, flops=10 ** 9, nbytes=4 * width * (3 * rows + rank))  9.16 us
    ppermute x3, starting transfers between devices, local(): lax.ppermute(x, 'leaf', down_pairs)  6.81 us
  transfers between devices with their start and end apart: 7, of which 0 were waited for; matrix products, arithmetic and copies ran while one was open for 10% of the time, Pallas kernels for 50%

profile of v1, /device:TPU:20, one launch (start us, length us, event | category | flops | bytes accessed | tf_op | source)
XLA Modules:
  0.0 274.3 jit_solution(12231559563841043763)
XLA Ops:
  6.5 0.9 constant_dynamic-slice_fusion.1
  7.5 0.9 constant_dynamic-slice_fusion
  8.4 0.0 copy-start.4
  8.4 0.0 copy-start.5
  8.4 0.0 copy-start.6
  8.4 3.6 %collective-permute-start = (f32[3,12288]{1,0:T(4,128)S(1)}, f32[3,12288]{1,0:T(4,128)S(1)}, u32[]{:S(2)}, u32[]{:S(2)}) collective-permute-start(f32[3,12288]{1,0:T(4,128)S(1)} %pad_maximum_fusion.1), channel_id=1, source_target_pairs={{0,4},{4,8},{8,12},{1,5},{5,9},{9,13},{2,6},{6,10},{10,14},{3,7},{... | collective-permute-start | bytes 442376 | tf_op jit(solution)/shard_map/ppermute | solution.py:432
  12.0 2.4 collective-permute-start.1
  14.4 3.5 %collective-permute-start.4 = (f32[16,32768]{1,0:T(8,128)}, f32[16,32768]{1,0:T(8,128)}, u32[]{:S(2)}, u32[]{:S(2)}) collective-permute-start(f32[16,32768]{1,0:T(8,128)} %refs_1_.1), channel_id=1, source_target_pairs={{0,4},{4,8},{8,12},{1,5},{5,9},{9,13},{2,6},{6,10},{10,14},{3,7},{... | collective-permute-start | bytes 6291464 | tf_op jit(solution)/shard_map/ppermute | solution.py:432
  17.9 2.4 collective-permute-start.5
  20.3 10.9 %shard_map.199.c_ref.refs_1_ = f32[16,16384]{1,0:T(8,128)} custom-call(f32[16,32768]{1,0:T(8,128)} %refs_1_.1, f32[32,32768]{1,0:T(8,128)} %b_ref.3), custom_call_target="tpu_custom_call" | custom-call | flops 1000000000 | bytes 6291456 | tf_op jit(solution)/shard_map/pallas_call | solution.py:117
  31.1 4.9 %collective-permute-start.2 = (f32[16,16384]{1,0:T(8,128)}, f32[16,16384]{1,0:T(8,128)S(1)}, u32[]{:S(2)}, u32[]{:S(2)}) collective-permute-start(f32[16,16384]{1,0:T(8,128)} %shard_map.199.c_ref.refs_1_), channel_id=1, source_target_pairs={{0,4},{4,8},{8,12},{1,5},{5,9},{9,13},{2,6},{6,10},{10,14},{3,7},{... | collective-permute-start | bytes 3145736 | tf_op jit(solution)/shard_map/ppermute | solution.py:432
  36.3 0.7 fusion.122
  36.9 0.1 select_reduce_fusion.8
  37.1 1.1 select_reduce_fusion.1
  38.2 0.1 multiply_reduce_fusion.2
  38.3 0.1 select_reduce_fusion.14
  38.4 1.2 fusion.51
  39.6 0.6 iota_compare_fusion.27
  40.2 0.1 select_reduce_fusion.9
  40.4 1.1 select_reduce_fusion.3
  41.5 1.2 fusion.45
  42.7 0.7 iota_compare_fusion.29
  43.4 0.7 fusion.127
  44.1 0.1 select_reduce_fusion.10
  44.2 1.1 select_reduce_fusion.5
  45.4 0.6 iota_compare_fusion.30
  46.0 0.1 select_reduce_fusion.11
  46.2 1.1 select_reduce_fusion.7
  47.3 0.6 iota_compare_fusion.31
  47.9 0.1 constant_dynamic-slice_fusion.2
  48.0 0.3 multiply_reduce_fusion
  48.3 0.3 select_reduce_fusion.12
  48.6 1.2 fusion.33
  49.8 1.2 fusion.39
  51.1 2.1 collective-permute-start.3
  53.2 0.9 pad_maximum_fusion
  54.1 0.0 all-gather.4.cloned.1.call-update
  54.2 12.1 %shard_map.200 = f32[16,32]{1,0:T(8,128)} custom-call(f32[16,16384]{1,0:T(8,128)} %shard_map.199.c_ref.refs_1_, f32[32,32704]{1,0:T(8,128)} %e_ref.3), custom_call_target="tpu_custom_call" | custom-call | flops 1000000000 | bytes 5242880 | tf_op jit(solution)/shard_map/pallas_call | solution.py:175
  68.1 1.1 pad.23.place_ref.refs_0_
  69.2 0.8 pad.20.place_ref.refs_0_
  70.8 25.6 %all-gather.1 = f32[4,32,16]{1,2,0:T(8,128)S(1)} all-gather(f32[1,32,16]{1,2,0:T(8,128)S(1)} %bitcast.97), channel_id=1, replica_groups=mesh['groups'=2,'leaf'=4,'level'=2,'sub'=2] {'leaf'}, dimensions={0}, use_global_device_ids=true | all-gather | bytes 10240 | tf_op jit(solution)/shard_map/all_gather | solution.py:473
  96.3 0.1 reshape.329
  96.4 0.8 fusion.80.r_ref
  97.3 17.0 %shard_map.201.d_ref = f32[16,16384]{1,0:T(8,128)} custom-call(f32[16,32]{1,0:T(8,128)} %fusion.80.r_ref, f32[32,32704]{1,0:T(8,128)} %e_ref.3), custom_call_target="tpu_custom_call" | custom-call | flops 1000000000 | bytes 5242880 | tf_op jit(solution)/shard_map/pallas_call | solution.py:215
  114.3 0.6 pad_add_fusion.3.list_ref
  114.9 0.6 pad_add_fusion.2.list_ref
  115.5 0.6 pad_add_fusion.1.list_ref
  116.1 0.6 pad_add_fusion.list_ref
  116.7 31.9 %shard_map.204.refs_4_ = f32[16,32768]{1,0:T(8,128)} custom-call(s32[5121]{0:T(1024)} %pad_add_fusion.3.list_ref, bf16[16,16]{1,0:T(8,128)(2,1)} %constant.153.clone.pick_s_ref, bf16[16,16]{1,0:T(8,128)(2,1)} %constant.154.clone.pick_t_ref, bf16[128,128]{1,0:T(8,128)(2,1)} %constant.155.clone.eye_ref, f32[8,32768]{1,0:T(8,128)} %pad.23.place_ref.refs_0_, ...), custom_call_target="tpu_custom_call" | custom-call | flops 4000000000 | bytes 30000000 | tf_op jit(solution)/shard_map/pallas_call | solution.py:410
  148.6 31.2 %shard_map.202.refs_4_ = f32[16,16384]{1,0:T(8,128)} custom-call(s32[9217]{0:T(1024)} %pad_add_fusion.1.list_ref, bf16[16,16]{1,0:T(8,128)(2,1)} %constant.153.clone.pick_s_ref, bf16[16,16]{1,0:T(8,128)(2,1)} %constant.154.clone.pick_t_ref, bf16[128,128]{1,0:T(8,128)(2,1)} %constant.155.clone.eye_ref, f32[8,16384]{1,0:T(8,128)} %pad.20.place_ref.refs_0_, ...), custom_call_target="tpu_custom_call" | custom-call | flops 4000000000 | bytes 30000000 | tf_op jit(solution)/shard_map/pallas_call | solution.py:410
  179.8 2.2 copy.78
  182.0 0.1 slice_bitcast_fusion
  182.1 0.3 copy.70
  182.4 1.0 pad.24.refs_0_
  183.4 0.3 copy.71
  183.7 1.0 pad.25.refs_1_
  184.7 0.1 copy.66
  184.9 0.8 pad.21.refs_0_
  185.7 0.1 copy.67
  185.9 0.8 pad.22.refs_1_
  186.7 1.0 copy-done.8
  187.7 34.4 %shard_map.203.c_ref = f32[16,16384]{1,0:T(8,128)} custom-call(s32[9217]{0:T(1024)} %pad_add_fusion.list_ref, bf16[16,16]{1,0:T(8,128)(2,1)} %constant.153.clone.pick_s_ref, bf16[16,16]{1,0:T(8,128)(2,1)} %constant.154.clone.pick_t_ref, bf16[128,128]{1,0:T(8,128)(2,1)} %constant.155.clone.eye_ref, f32[8,16384]{1,0:T(8,128)} %pad.20.place_ref.refs_0_, ...), custom_call_target="tpu_custom_call" | custom-call | flops 4000000000 | bytes 30000000 | tf_op jit(solution)/shard_map/pallas_call | solution.py:410
  222.1 36.2 %shard_map.205.n_ref = f32[16,32768]{1,0:T(8,128)} custom-call(s32[5121]{0:T(1024)} %pad_add_fusion.2.list_ref, bf16[16,16]{1,0:T(8,128)(2,1)} %constant.153.clone.pick_s_ref, bf16[16,16]{1,0:T(8,128)(2,1)} %constant.154.clone.pick_t_ref, bf16[128,128]{1,0:T(8,128)(2,1)} %constant.155.clone.eye_ref, f32[8,32768]{1,0:T(8,128)} %pad.23.place_ref.refs_0_, ...), custom_call_target="tpu_custom_call" | custom-call | flops 4000000000 | bytes 30000000 | tf_op jit(solution)/shard_map/pallas_call | solution.py:410
  258.3 9.2 %shard_map.206 = f32[16,32768]{1,0:T(8,128)} custom-call(f32[16,16384]{1,0:T(8,128)} %shard_map.201.d_ref, f32[16,16384]{1,0:T(8,128)} %shard_map.203.c_ref, f32[32,32768]{1,0:T(8,128)} %b_ref.3, f32[16,32768]{1,0:T(8,128)} %shard_map.205.n_ref), custom_call_target="tpu_custom_call" | custom-call | flops 1000000000 | bytes 10485760 | tf_op jit(solution)/shard_map/pallas_call | solution.py:141
  (59 shorter events, 0.5 us)
Async XLA Ops:
  6.5 173.3 %all-gather.4.cloned.1.call-start = ((), (), s32[]{:S(2)}) async-start(), calls=%async_computation | async-start | bytes 1966080 | tf_op jit(solution)/shard_map/all_gather | solution.py:445
  8.4 27.7 %copy-start.4 = (s32[512,16]{0,1:T(8,128)S(1)}, s32[512,16]{0,1:T(8,128)}, u32[]{:S(2)}) copy-start(s32[512,16]{0,1:T(8,128)} %param.29) | copy-start | bytes 98308
  8.4 27.8 %copy-start.5 = (s32[512,8]{0,1:T(8,128)S(1)}, s32[512,8]{0,1:T(8,128)}, u32[]{:S(2)}) copy-start(s32[512,8]{0,1:T(8,128)} %param.27) | copy-start | bytes 49156
  8.4 27.8 %copy-start.6 = (s32[512]{0:T(512)S(1)}, s32[512]{0:T(512)}, u32[]{:S(2)}) copy-start(s32[512]{0:T(512)} %param.28) | copy-start | bytes 6148
  8.4 42.7 %collective-permute-start = (f32[3,12288]{1,0:T(4,128)S(1)}, f32[3,12288]{1,0:T(4,128)S(1)}, u32[]{:S(2)}, u32[]{:S(2)}) collective-permute-start(f32[3,12288]{1,0:T(4,128)S(1)} %pad_maximum_fusion.1), channel_id=1, source_target_pairs={{0,4},{4,8},{8,12},{1,5},{5,9},{9,13},{2,6},{6,10},{10,14},{3,7},{... | collective-permute-start | bytes 442376 | tf_op jit(solution)/shard_map/ppermute | solution.py:432
  12.0 41.2 %collective-permute-start.1 = (f32[3,12288]{1,0:T(4,128)S(1)}, f32[3,12288]{1,0:T(4,128)S(1)}, u32[]{:S(2)}, u32[]{:S(2)}) collective-permute-start(f32[3,12288]{1,0:T(4,128)S(1)} %pad_maximum_fusion.1), channel_id=1, source_target_pairs={{4,0},{8,4},{12,8},{5,1},{9,5},{13,9},{6,2},{10,6},{14,10},{7,3},{... | collective-permute-start | bytes 442376 | tf_op jit(solution)/shard_map/ppermute | solution.py:432
  14.4 207.7 %collective-permute-start.4 = (f32[16,32768]{1,0:T(8,128)}, f32[16,32768]{1,0:T(8,128)}, u32[]{:S(2)}, u32[]{:S(2)}) collective-permute-start(f32[16,32768]{1,0:T(8,128)} %refs_1_.1), channel_id=1, source_target_pairs={{0,4},{4,8},{8,12},{1,5},{5,9},{9,13},{2,6},{6,10},{10,14},{3,7},{... | collective-permute-start | bytes 6291464 | tf_op jit(solution)/shard_map/ppermute | solution.py:432
  17.9 204.2 %collective-permute-start.5 = (f32[16,32768]{1,0:T(8,128)}, f32[16,32768]{1,0:T(8,128)}, u32[]{:S(2)}, u32[]{:S(2)}) collective-permute-start(f32[16,32768]{1,0:T(8,128)} %refs_1_.1), channel_id=1, source_target_pairs={{4,0},{8,4},{12,8},{5,1},{9,5},{13,9},{6,2},{10,6},{14,10},{7,3},{... | collective-permute-start | bytes 6291464 | tf_op jit(solution)/shard_map/ppermute | solution.py:432
  31.1 16.7 %copy-start.7 = (f32[3,128]{1,0:T(4,128)S(1)}, f32[3,128]{1,0:T(4,128)}, u32[]{:S(2)}) copy-start(f32[3,128]{1,0:T(4,128)} %param.26) | copy-start | bytes 4612
  31.1 155.6 %collective-permute-start.2 = (f32[16,16384]{1,0:T(8,128)}, f32[16,16384]{1,0:T(8,128)S(1)}, u32[]{:S(2)}, u32[]{:S(2)}) collective-permute-start(f32[16,16384]{1,0:T(8,128)} %shard_map.199.c_ref.refs_1_), channel_id=1, source_target_pairs={{0,4},{4,8},{8,12},{1,5},{5,9},{9,13},{2,6},{6,10},{10,14},{3,7},{... | collective-permute-start | bytes 3145736 | tf_op jit(solution)/shard_map/ppermute | solution.py:432
  42.7 8.4 %copy-start = (f32[16,16384]{1,0:T(8,128)S(1)}, f32[16,16384]{1,0:T(8,128)}, u32[]{:S(2)}) copy-start(f32[16,16384]{1,0:T(8,128)} %shard_map.199.c_ref.refs_1_) | copy-start | bytes 3145732
  51.1 135.6 %collective-permute-start.3 = (f32[16,16384]{1,0:T(8,128)S(1)}, f32[16,16384]{1,0:T(8,128)}, u32[]{:S(2)}, u32[]{:S(2)}) collective-permute-start(f32[16,16384]{1,0:T(8,128)S(1)} %copy-done), channel_id=1, source_target_pairs={{4,0},{8,4},{12,8},{5,1},{9,5},{13,9},{6,2},{10,6},{14,10},{7,3},{... | collective-permute-start | bytes 3145736 | tf_op jit(solution)/shard_map/ppermute | solution.py:432
  54.1 14.0 %copy-start.1 = (f32[3,32768]{1,0:T(4,128)S(1)}, f32[3,32768]{1,0:T(4,128)}, u32[]{:S(2)}) copy-start(f32[3,32768]{1,0:T(4,128)} %param.22) | copy-start | bytes 1179652
  54.1 15.1 %copy-start.2 = (f32[3,16384]{1,0:T(4,128)S(1)}, f32[3,16384]{1,0:T(4,128)}, u32[]{:S(2)}) copy-start(f32[3,16384]{1,0:T(4,128)} %param.25) | copy-start | bytes 589828
  66.2 4.5 %copy-start.3 = (f32[16,32]{1,0:T(8,128)S(1)}, f32[16,32]{1,0:T(8,128)}, u32[]{:S(2)}) copy-start(f32[16,32]{1,0:T(8,128)} %shard_map.200) | copy-start | bytes 6148
  186.7 1.0 copy-start.8
Sparse Core Ops, SparseCore 0:
  54.2 21.9 all-gather.3

commit v2 on v1

--- a/solution.py
+++ b/solution.py
@@ -82,7 +82,7 @@
     return [pl.BlockSpec(memory_space=pltpu.VMEM)] * n
 
 
-def call(body, out_shape, n_in, scratch=(), flops=0, nbytes=0, prefetch=False):
+def call(body, out_shape, n_in, scratch=(), nbytes=0, prefetch=False):
     specs = ([pl.BlockSpec(memory_space=pltpu.SMEM)] if prefetch else []) + whole(n_in)
     return pl.pallas_call(
         body,
@@ -91,7 +91,7 @@
         out_specs=pl.BlockSpec(memory_space=pltpu.VMEM),
         scratch_shapes=list(scratch),
         compiler_params=pltpu.CompilerParams(vmem_limit_bytes=VMEM_LIMIT),
-        cost_estimate=pl.CostEstimate(flops=flops, bytes_accessed=nbytes, transcendentals=0),
+        cost_estimate=pl.CostEstimate(flops=0, bytes_accessed=nbytes, transcendentals=0),
     )
 
 
@@ -114,7 +114,7 @@
         in_chunks(width // span, 8, run)
 
     out = jax.ShapeDtypeStruct((rows, width // leaf_pts * rank), f32)
-    return call(body, out, 2, flops=10**9, nbytes=4 * width * (rows + rank))(rhs, basis)
+    return call(body, out, 2, nbytes=4 * 10**7)(rhs, basis)
 
 
 def leaf_product(down, couple, basis, near, leaf_pts):
@@ -138,7 +138,7 @@
         in_chunks(width // span, 8, run)
 
     out = jax.ShapeDtypeStruct((rows, width), f32)
-    return call(body, out, 4, flops=10**9, nbytes=4 * width * (3 * rows + rank))(
+    return call(body, out, 4, nbytes=4 * 10**7)(
         down, couple, basis, near
     )
 
@@ -177,8 +177,7 @@
         jax.ShapeDtypeStruct((rows, rank), f32),
         2,
         [pltpu.VMEM((2, rows, width), f32)],
-        flops=10**9,
-        nbytes=4 * width * (rows + 2 * rank),
+        nbytes=4 * 10**7,
     )(coef, transfer)
 
 
@@ -217,8 +216,7 @@
         jax.ShapeDtypeStruct((rows, width), f32),
         2,
         [pltpu.VMEM((2, rows, width), f32)],
-        flops=10**9,
-        nbytes=4 * width * (rows + 2 * rank),
+        nbytes=4 * 10**7,
     )(root, transfer)
 
 
@@ -284,7 +282,7 @@
     return jnp.concatenate([target, sources.T.reshape(-1), steps[None]]), items
 
 
-def pair_sums(listing, items, place, coords, sources, before, leaves, pts):
+def pair_sums(listing, items, place, coords, sources, leaves, pts):
     rows = sources[0].shape[0]
     width = leaves * pts
     per = LANES // pts
@@ -299,9 +297,7 @@
     def body(list_ref, pick_s_ref, pick_t_ref, eye_ref, place_ref, *refs):
         coord_refs = refs[:pieces]
         x_refs = refs[pieces : 2 * pieces]
-        more = refs[2 * pieces :]
-        base_ref = more[0] if before is not None else None
-        o_ref, tab, targets_tab, acc = more[-4:]
+        o_ref, tab, targets_tab, acc = refs[2 * pieces :]
         lane = lax.broadcasted_iota(i32, (1, LANES), 1) // pts
 
         def fill_targets(first, n):
@@ -396,8 +392,7 @@
                         out = one if j == 0 else jnp.where(lane == j, one, out)
                     outs.append(out)
             for c, out in enumerate(outs):
-                here = at(start + c, LANES)
-                o_ref[:, here] = out if base_ref is None else out + base_ref[:, here]
+                o_ref[:, at(start + c, LANES)] = out
 
         in_chunks(width // LANES, 16, lay)
 
@@ -406,14 +401,13 @@
         pltpu.VMEM((leaves, pts, FEATS), bf16),
         pltpu.VMEM((leaves, pts, 2 * rows) if narrow else (leaves, rows, LANES), f32),
     ]
-    args = [listing, *consts, place, *coords, *sources] + ([before] if before is not None else [])
+    args = [listing, *consts, place, *coords, *sources]
     return call(
         body,
         jax.ShapeDtypeStruct((rows, width), f32),
         len(args) - 1,
         scratch,
-        flops=4 * 10**9,
-        nbytes=3 * 10**7,
+        nbytes=15 * 10**7,
         prefetch=True,
     )(*args)
 
@@ -451,40 +445,52 @@
     halo_rhs = both_ways(rhs)
     halo_coef = both_ways(coef)
 
-    anchor = owner * leaves
-
-    def lists(src, live, group):
-        place = src - anchor
-        own = (place >= 0) & (place < leaves)
-        inside = work_list(place, live & own, group, leaves)
-        outside = jnp.where(place < 0, place + leaves, place)
-        return inside, work_list(outside, live & ~own, group, 2 * leaves)
-
+    anchor = (owner - 1) * leaves
     live = jnp.arange(near_max, dtype=i32)[None, :] < near_count[:, None]
-    near_in, near_out = lists(near_src, live, WIDE * LANES // leaf_pts)
-    far_in, far_out = lists(far_src, jnp.ones(far_src.shape, bool), WIDE * LANES // rank)
+    near_list = work_list(near_src - anchor, live, WIDE * LANES // leaf_pts, 3 * leaves)
+    far_live = jnp.ones(far_src.shape, bool)
+    far_list = work_list(far_src - anchor, far_live, WIDE * LANES // rank, 3 * leaves)
+
+    root = tree_up(coef, transfer, leaves)
+    parts, origins = [], []
+    for s in range(2, size):
+        rise, fall = [(i, i + s) for i in range(size - s)], [(i + s, i) for i in range(size - s)]
+        if 2 * s >= size:
+            parts.append(lax.ppermute(root, "leaf", rise + fall))
+            origins.append(jnp.where(owner >= s, owner - s, owner + s))
+        else:
+            parts += [lax.ppermute(root, "leaf", rise), lax.ppermute(root, "leaf", fall)]
+            origins += [owner - s, owner + s]
 
     own_points, own_proxies = eight_rows(points), eight_rows(leaf_proxies)
-    near = pair_sums(*near_in, own_points, [own_points], [rhs], None, leaves, leaf_pts)
-    couple = pair_sums(*far_in, own_proxies, [own_proxies], [coef], None, leaves, rank)
-
-    root = tree_up(coef, transfer, leaves)
+    near = pair_sums(
+        *near_list,
+        own_points,
+        [eight_rows(halo_points[0]), own_points, eight_rows(halo_points[1])],
+        [halo_rhs[0], rhs, halo_rhs[1]],
+        leaves,
+        leaf_pts,
+    )
+
+    parts, near = lax.optimization_barrier((parts, near))
     own_proxy = lax.dynamic_slice_in_dim(root_proxies, owner * rank, rank, 1)
-    piece = lax.all_gather(root, "leaf", axis=1, tiled=True)
-    dist = (own_proxy[0][:, None] - root_proxies[0][None, :]) ** 2
-    dist = dist + (own_proxy[1][:, None] - root_proxies[1][None, :]) ** 2
-    dist = dist + (own_proxy[2][:, None] - root_proxies[2][None, :]) ** 2
-    source_owner = jnp.arange(piece.shape[1], dtype=i32) // rank
-    far_mask = (jnp.abs(source_owner - owner) >= 2).astype(f32)
-    kernel = jnp.exp(-dist / spread_sq) * far_mask[None, :]
-    top = jnp.einsum("aj,rj->ra", kernel, piece, precision=highest)
+    top = jnp.zeros((rows, rank), f32)
+    for part, origin in zip(parts, origins):
+        there = (origin >= 0) & (origin < size)
+        start = jnp.clip(origin, 0, size - 1) * rank
+        proxy = lax.dynamic_slice_in_dim(root_proxies, start, rank, 1)
+        dist = jnp.sum((own_proxy[:, :, None] - proxy[:, None, :]) ** 2, axis=0)
+        kernel = jnp.where(there, jnp.exp(-dist / spread_sq), 0.0)
+        top = top + jnp.einsum("aj,rj->ra", kernel, part, precision=highest)
     down = tree_down(top, transfer, leaves)
 
-    halo_points = [eight_rows(halo_points[i]) for i in range(2)]
-    halo_proxies = [eight_rows(halo_proxies[i]) for i in range(2)]
-    near = pair_sums(*near_out, own_points, halo_points, list(halo_rhs), near, leaves, leaf_pts)
     couple = pair_sums(
-        *far_out, own_proxies, halo_proxies, list(halo_coef), couple, leaves, rank
+        *far_list,
+        own_proxies,
+        [eight_rows(halo_proxies[0]), own_proxies, eight_rows(halo_proxies[1])],
+        [halo_coef[0], coef, halo_coef[1]],
+        leaves,
+        rank,
     )
     return leaf_product(down, couple, basis, near, leaf_pts)
 

time: 277 us -> 219 us (0.79)
  the two profiles are of different devices: /device:TPU:20 before, /device:TPU:13 now
where the time goes in v2:
time: 219 us; the launch traced here: 221 us
  Pallas kernels  147 us (67%)
  starting transfers between devices  20.7 us (9%)
  waiting for transfers between devices  15.7 us (7%)
  between operations  14.3 us (7%)
  local copies, waits for them, and re-layouts  11.8 us (5%)
  other arithmetic  8 us (4%)
  matrix products  3.33 us (2%)
    pallas_call x2, Pallas kernels, pair_sums(): call(body, jax.ShapeDtypeStruct((rows, width), f32), len(args) - 1, scrat...  98.3 us
    pallas_call x1, Pallas kernels, tree_down(): call(body, jax.ShapeDtypeStruct((rows, width), f32), 2, [pltpu.VMEM((2, r...  16.9 us
    all_gather x1, waiting for transfers between devices, local(): coords = lax.all_gather(share, ('level', 'sub'), axis=0)  15.7 us
    pallas_call x1, Pallas kernels, tree_up(): call(body, jax.ShapeDtypeStruct((rows, rank), f32), 2, [pltpu.VMEM((2, ro...  12 us
    pallas_call x1, Pallas kernels, leaf_coefs(): return call(body, out, 2, nbytes=4 * 10 ** 7)(rhs, basis)  10.9 us
    ppermute x3, starting transfers between devices, local(): lax.ppermute(x, 'leaf', up)  9.69 us
    pallas_call x1, Pallas kernels, leaf_product(): return call(body, out, 4, nbytes=4 * 10 ** 7)(down, couple, basis, near)  9.16 us
    ppermute x3, starting transfers between devices, local(): lax.ppermute(x, 'leaf', down_pairs)  8.11 us
  transfers between devices with their start and end apart: 9, of which 1 were waited for; matrix products, arithmetic and copies ran while one was open for 9% of the time, Pallas kernels for 55%

profile of v2, /device:TPU:13, one launch (start us, length us, event | category | flops | bytes accessed | tf_op | source)
XLA Modules:
  0.0 221.2 jit_solution(3191578776909776751)
XLA Ops:
  6.5 0.0 all-gather.3.cloned.1.call-start
  6.5 0.9 constant_dynamic-slice_fusion.3
  7.4 0.9 constant_dynamic-slice_fusion.4
  8.3 0.7 pad_maximum_fusion.1
  9.1 2.2 collective-permute-start.3
  11.3 3.2 %collective-permute-start.2 = (f32[3,12288]{1,0:T(4,128)}, f32[3,12288]{1,0:T(4,128)}, u32[]{:S(2)}, u32[]{:S(2)}) collective-permute-start(f32[3,12288]{1,0:T(4,128)} %pad_maximum_fusion.1), channel_id=1, source_target_pairs={{0,4},{4,8},{8,12},{1,5},{5,9},{9,13},{2,6},{6,10},{10,14},{3,7},{... | collective-permute-start | bytes 442376 | tf_op jit(solution)/shard_map/ppermute | solution.py:426
  14.5 10.9 %shard_map.145.c_ref.refs_4_ = f32[16,16384]{1,0:T(8,128)} custom-call(f32[16,32768]{1,0:T(8,128)} %refs_4_.1, f32[32,32768]{1,0:T(8,128)} %b_ref.3), custom_call_target="tpu_custom_call" | custom-call | bytes 40000000 | tf_op jit(solution)/shard_map/pallas_call | solution.py:117
  25.4 2.7 %collective-permute-start.7 = (f32[16,16384]{1,0:T(8,128)}, f32[16,16384]{1,0:T(8,128)S(1)}, u32[]{:S(2)}, u32[]{:S(2)}) collective-permute-start(f32[16,16384]{1,0:T(8,128)} %shard_map.145.c_ref.refs_4_), channel_id=1, source_target_pairs={{4,0},{8,4},{12,8},{5,1},{9,5},{13,9},{6,2},{10,6},{14,10},{7,3},{... | collective-permute-start | bytes 3145736 | tf_op jit(solution)/shard_map/ppermute | solution.py:426
  28.1 3.1 %collective-permute-start.6 = (f32[16,16384]{1,0:T(8,128)}, f32[16,16384]{1,0:T(8,128)}, u32[]{:S(2)}, u32[]{:S(2)}) collective-permute-start(f32[16,16384]{1,0:T(8,128)} %shard_map.145.c_ref.refs_4_), channel_id=1, source_target_pairs={{0,4},{4,8},{8,12},{1,5},{5,9},{9,13},{2,6},{6,10},{10,14},{3,7},{... | collective-permute-start | bytes 3145736 | tf_op jit(solution)/shard_map/ppermute | solution.py:426
  31.2 3.4 %collective-permute-start.4 = (f32[16,32768]{1,0:T(8,128)S(1)}, f32[16,32768]{1,0:T(8,128)}, u32[]{:S(2)}, u32[]{:S(2)}) collective-permute-start(f32[16,32768]{1,0:T(8,128)S(1)} %copy-done), channel_id=1, source_target_pairs={{0,4},{4,8},{8,12},{1,5},{5,9},{9,13},{2,6},{6,10},{10,14},{3,7},{... | collective-permute-start | bytes 6291464 | tf_op jit(solution)/shard_map/ppermute | solution.py:426
  34.6 0.0 copy-done.7
  34.7 0.6 fusion.66
  35.3 0.6 iota_compare_fusion.17
  35.8 0.1 select_reduce_fusion.5
  36.0 1.1 select_reduce_fusion.3
  37.1 0.1 multiply_reduce_fusion
  37.3 1.2 fusion.24
  38.6 0.0 copy-start.2
  38.6 12.0 %shard_map.146 = f32[16,32]{1,0:T(8,128)} custom-call(f32[16,16384]{1,0:T(8,128)} %shard_map.145.c_ref.refs_4_, f32[32,32704]{1,0:T(8,128)} %e_ref.3), custom_call_target="tpu_custom_call" | custom-call | bytes 40000000 | tf_op jit(solution)/shard_map/pallas_call | solution.py:175
  50.6 0.0 collective-permute-done.3
  50.6 3.2 %collective-permute-start.5 = (f32[16,32768]{1,0:T(8,128)S(1)}, f32[16,32768]{1,0:T(8,128)}, u32[]{:S(2)}, u32[]{:S(2)}) collective-permute-start(f32[16,32768]{1,0:T(8,128)S(1)} %copy-done), channel_id=1, source_target_pairs={{4,0},{8,4},{12,8},{5,1},{9,5},{13,9},{6,2},{10,6},{14,10},{7,3},{... | collective-permute-start | bytes 6291464 | tf_op jit(solution)/shard_map/ppermute | solution.py:426
  53.8 0.0 collective-permute-done.2
  53.8 0.7 collective-permute-start.1
  54.5 1.9 pad_maximum_fusion
  56.4 0.0 all-gather.3.cloned.1.call-update
  56.4 0.2 select_reduce_fusion.4
  57.1 0.0 copy-done.2
  57.1 0.0 copy-start.4
  57.1 0.8 pad.23.place_ref.refs_1_
  58.0 2.1 pad.20.place_ref.refs_1_
  60.1 0.1 convert_reduce_fusion
  60.2 0.1 select_reduce_fusion.6
  60.3 1.1 select_reduce_fusion.1
  61.4 1.2 fusion.18
  62.7 0.0 copy-done.4
  62.7 0.1 constant_dynamic-slice_fusion
  62.8 0.6 pad_add_fusion.1.list_ref
  63.4 0.1 multiply_reduce_fusion.2
  63.5 0.6 pad_add_fusion.list_ref
  64.1 15.7 %all-gather.3.cloned.1.call-done = f32[8,3,12288]{2,1,0:T(4,128)} async-done(((f32[2,3,12288]{2,1,0:T(4,128)}), f32[8,3,12288]{2,1,0:T(4,128)}) %all-gather.3.cloned.1.call-update) | async-done | bytes 1179664 | tf_op jit(solution)/shard_map/all_gather | solution.py:439
  79.8 2.2 copy.35
  82.0 0.1 slice_bitcast_fusion
  82.1 0.0 collective-permute-done.7.refs_5_
  82.1 2.2 collective-permute-start
  84.3 0.1 copy.31
  84.4 0.3 copy.28
  84.7 0.8 pad.25.refs_2_
  85.6 0.1 copy.30
  85.7 0.8 pad.24.refs_0_
  86.5 0.0 copy-done.1
  86.5 1.1 pad.22.refs_2_
  87.6 0.3 copy.27
  87.9 1.1 pad.21.refs_0_
  89.0 0.0 collective-permute-done.6.refs_3_
  89.0 46.0 %shard_map.149.c_ref = f32[16,16384]{1,0:T(8,128)} custom-call(s32[9217]{0:T(1024)} %pad_add_fusion.list_ref, bf16[16,16]{1,0:T(8,128)(2,1)} %constant.173.clone.pick_s_ref, bf16[16,16]{1,0:T(8,128)(2,1)} %constant.174.clone.pick_t_ref, bf16[128,128]{1,0:T(8,128)(2,1)} %constant.175.clone.eye_ref, f32[8,16384]{1,0:T(8,128)} %pad.23.place_ref.refs_1_, ...), custom_call_target="tpu_custom_call" | custom-call | bytes 150000000 | tf_op jit(solution)/shard_map/pallas_call | solution.py:405
  135.0 0.0 collective-permute-done.4.refs_3_
  135.0 0.0 collective-permute-done.5.refs_5_
  135.0 52.3 %shard_map.147.n_ref = f32[16,32768]{1,0:T(8,128)} custom-call(s32[5121]{0:T(1024)} %pad_add_fusion.1.list_ref, bf16[16,16]{1,0:T(8,128)(2,1)} %constant.173.clone.pick_s_ref, bf16[16,16]{1,0:T(8,128)(2,1)} %constant.174.clone.pick_t_ref, bf16[128,128]{1,0:T(8,128)(2,1)} %constant.175.clone.eye_ref, f32[8,32768]{1,0:T(8,128)} %pad.20.place_ref.refs_1_, ...), custom_call_target="tpu_custom_call" | custom-call | bytes 150000000 | tf_op jit(solution)/shard_map/pallas_call | solution.py:405
  187.3 0.0 collective-permute-done.1
  187.3 0.0 collective-permute-done
  187.3 0.1 fusion.36
  187.4 0.8 convolution_add_fusion.r_ref
  188.2 16.9 %shard_map.148.d_ref = f32[16,16384]{1,0:T(8,128)} custom-call(f32[16,32]{1,0:T(8,128)} %convolution_add_fusion.r_ref, f32[32,32704]{1,0:T(8,128)} %e_ref.3), custom_call_target="tpu_custom_call" | custom-call | bytes 40000000 | tf_op jit(solution)/shard_map/pallas_call | solution.py:214
  205.1 9.2 %shard_map.150 = f32[16,32768]{1,0:T(8,128)} custom-call(f32[16,16384]{1,0:T(8,128)} %shard_map.148.d_ref, f32[16,16384]{1,0:T(8,128)} %shard_map.149.c_ref, f32[32,32768]{1,0:T(8,128)} %b_ref.3, f32[16,32768]{1,0:T(8,128)} %shard_map.147.n_ref), custom_call_target="tpu_custom_call" | custom-call | bytes 40000000 | tf_op jit(solution)/shard_map/pallas_call | solution.py:141
  (28 shorter events, 0.2 us)
Async XLA Ops:
  6.5 73.3 %all-gather.3.cloned.1.call-start = ((), (), s32[]{:S(2)}) async-start(), calls=%async_computation | async-start | bytes 1966080 | tf_op jit(solution)/shard_map/all_gather | solution.py:439
  9.0 22.1 %copy-start = (f32[16,32768]{1,0:T(8,128)S(1)}, f32[16,32768]{1,0:T(8,128)}, u32[]{:S(2)}) copy-start(f32[16,32768]{1,0:T(8,128)} %refs_4_.1) | copy-start | bytes 6291460
  9.0 25.6 %copy-start.7 = (s32[512]{0:T(512)S(1)}, s32[512]{0:T(512)}, u32[]{:S(2)}) copy-start(s32[512]{0:T(512)} %param.22) | copy-start | bytes 6148
  9.0 28.0 %copy-start.5 = (s32[512,8]{0,1:T(8,128)S(1)}, s32[512,8]{0,1:T(8,128)}, u32[]{:S(2)}) copy-start(s32[512,8]{0,1:T(8,128)} %param.21) | copy-start | bytes 49156
  9.1 29.5 %copy-start.3 = (s32[512,16]{0,1:T(8,128)S(1)}, s32[512,16]{0,1:T(8,128)}, u32[]{:S(2)}) copy-start(s32[512,16]{0,1:T(8,128)} %param.23) | copy-start | bytes 98308
  9.1 41.6 %collective-permute-start.3 = (f32[3,12288]{1,0:T(4,128)}, f32[3,12288]{1,0:T(4,128)}, u32[]{:S(2)}, u32[]{:S(2)}) collective-permute-start(f32[3,12288]{1,0:T(4,128)} %pad_maximum_fusion.1), channel_id=1, source_target_pairs={{4,0},{8,4},{12,8},{5,1},{9,5},{13,9},{6,2},{10,6},{14,10},{7,3},{... | collective-permute-start | bytes 442376 | tf_op jit(solution)/shard_map/ppermute | solution.py:426
  11.3 42.6 %collective-permute-start.2 = (f32[3,12288]{1,0:T(4,128)}, f32[3,12288]{1,0:T(4,128)}, u32[]{:S(2)}, u32[]{:S(2)}) collective-permute-start(f32[3,12288]{1,0:T(4,128)} %pad_maximum_fusion.1), channel_id=1, source_target_pairs={{0,4},{4,8},{8,12},{1,5},{5,9},{9,13},{2,6},{6,10},{10,14},{3,7},{... | collective-permute-start | bytes 442376 | tf_op jit(solution)/shard_map/ppermute | solution.py:426
  25.4 56.7 %collective-permute-start.7 = (f32[16,16384]{1,0:T(8,128)}, f32[16,16384]{1,0:T(8,128)S(1)}, u32[]{:S(2)}, u32[]{:S(2)}) collective-permute-start(f32[16,16384]{1,0:T(8,128)} %shard_map.145.c_ref.refs_4_), channel_id=1, source_target_pairs={{4,0},{8,4},{12,8},{5,1},{9,5},{13,9},{6,2},{10,6},{14,10},{7,3},{... | collective-permute-start | bytes 3145736 | tf_op jit(solution)/shard_map/ppermute | solution.py:426
  28.1 60.9 %collective-permute-start.6 = (f32[16,16384]{1,0:T(8,128)}, f32[16,16384]{1,0:T(8,128)}, u32[]{:S(2)}, u32[]{:S(2)}) collective-permute-start(f32[16,16384]{1,0:T(8,128)} %shard_map.145.c_ref.refs_4_), channel_id=1, source_target_pairs={{0,4},{4,8},{8,12},{1,5},{5,9},{9,13},{2,6},{6,10},{10,14},{3,7},{... | collective-permute-start | bytes 3145736 | tf_op jit(solution)/shard_map/ppermute | solution.py:426
  31.2 103.8 %collective-permute-start.4 = (f32[16,32768]{1,0:T(8,128)S(1)}, f32[16,32768]{1,0:T(8,128)}, u32[]{:S(2)}, u32[]{:S(2)}) collective-permute-start(f32[16,32768]{1,0:T(8,128)S(1)} %copy-done), channel_id=1, source_target_pairs={{0,4},{4,8},{8,12},{1,5},{5,9},{9,13},{2,6},{6,10},{10,14},{3,7},{... | collective-permute-start | bytes 6291464 | tf_op jit(solution)/shard_map/ppermute | solution.py:426
  38.6 18.6 %copy-start.2 = (f32[3,16384]{1,0:T(4,128)S(1)}, f32[3,16384]{1,0:T(4,128)}, u32[]{:S(2)}) copy-start(f32[3,16384]{1,0:T(4,128)} %param.19) | copy-start | bytes 589828
  50.6 84.3 %collective-permute-start.5 = (f32[16,32768]{1,0:T(8,128)S(1)}, f32[16,32768]{1,0:T(8,128)}, u32[]{:S(2)}, u32[]{:S(2)}) collective-permute-start(f32[16,32768]{1,0:T(8,128)S(1)} %copy-done), channel_id=1, source_target_pairs={{4,0},{8,4},{12,8},{5,1},{9,5},{13,9},{6,2},{10,6},{14,10},{7,3},{... | collective-permute-start | bytes 6291464 | tf_op jit(solution)/shard_map/ppermute | solution.py:426
  53.8 133.5 %collective-permute-start.1 = (f32[16,32]{1,0:T(8,128)}, f32[16,32]{1,0:T(8,128)S(1)}, u32[]{:S(2)}, u32[]{:S(2)}) collective-permute-start(f32[16,32]{1,0:T(8,128)} %shard_map.146), channel_id=1, source_target_pairs={{0,12},{12,0},{1,13},{13,1},{2,14},{14,2},{3,15},{15,3},{16,28},{2... | collective-permute-start | bytes 6152 | tf_op jit(solution)/shard_map/ppermute | solution.py:459
  57.1 5.6 %copy-start.4 = (f32[3,128]{1,0:T(4,128)S(1)}, f32[3,128]{1,0:T(4,128)}, u32[]{:S(2)}) copy-start(f32[3,128]{1,0:T(4,128)} %param.20) | copy-start | bytes 4612
  79.8 2.3 %copy-start.6 = (f32[16,32]{1,0:T(8,128)S(1)}, f32[16,32]{1,0:T(8,128)}, u32[]{:S(2)}) copy-start(f32[16,32]{1,0:T(8,128)} %shard_map.146) | copy-start | bytes 6148
  82.1 4.5 %copy-start.1 = (f32[16,16384]{1,0:T(8,128)}, f32[16,16384]{1,0:T(8,128)S(1)}, u32[]{:S(2)}) copy-start(f32[16,16384]{1,0:T(8,128)S(1)} %collective-permute-done.7.refs_5_) | copy-start | bytes 3145732
  82.1 105.2 %collective-permute-start = (f32[16,32]{1,0:T(8,128)S(1)}, f32[16,32]{1,0:T(8,128)S(1)}, u32[]{:S(2)}, u32[]{:S(2)}) collective-permute-start(f32[16,32]{1,0:T(8,128)S(1)} %copy-done.6), channel_id=1, source_target_pairs={{0,8},{4,12},{8,0},{12,4},{1,9},{5,13},{9,1},{13,5},{2,10},{6,14},... | collective-permute-start | bytes 6152 | tf_op jit(solution)/shard_map/ppermute | solution.py:459
Sparse Core Ops, SparseCore 0:
  56.5 23.2 all-gather.2
